TPU v7x, 32 devices: a whole 2x2x4 slice. The times are simulated.
32 devices in a mesh: ctx: 8 (over z, y), tp: 4 (over x, core).
Axes of the slice: x: 2, y: 2, z: 4, core: 2. Of those that a mesh axis runs over, the one named last changes fastest.
Arguments:
- query_proj: bfloat16 [1024, 4096], P('ctx', 'tp'), may hold values from -6 to 6
- key_proj: bfloat16 [1024, 4096], P('ctx', 'tp'), may hold values from -6 to 6
- value_proj: bfloat16 [1024, 4096], P('ctx', 'tp'), may hold values from -6 to 6
- filters: float32 [256, 128], P('tp'), may hold values from -0.5 to 0.5
- skip_gain: float32 [4096], P('tp'), may hold values from -1 to 1
- out_grad: bfloat16 [1024, 4096], P('ctx', 'tp'), may hold values from -6 to 6
- w_out: bfloat16 [4096, 4096], P('tp'), may hold values from -0.09375 to 0.09375
Outputs:
- query_grad: bfloat16 [1024, 4096], P('ctx', 'tp')
- key_grad: bfloat16 [1024, 4096], P('ctx', 'tp')
- value_grad: bfloat16 [1024, 4096], P('ctx', 'tp')
- filter_grad: float32 [256, 128], P('tp')
- skip_grad: float32 [4096], P('tp')
All inputs are finite; a program needn't handle non-finite values.
Results may differ from a plain program's by a relative error of at most 0.0075.
Values may be sent and summed in bfloat16 or wider, within the bound.
A program may use at most 128 MiB of HBM per device.

v0:
```python
import jax
import jax.numpy as jnp
from jax import lax
from jax.sharding import PartitionSpec as P


def passed_along(block, axis, distance):
    devices = range(lax.axis_size(axis))
    route = [(i - distance, i) for i in devices if i - distance in devices]
    return lax.ppermute(block, axis, route)


def blocks_of(extended, width):
    count = (extended.shape[0] - width) // width
    channels = extended.shape[1]
    first = extended[:-width].reshape(count, width, channels)
    second = extended[width:].reshape(count, width, channels)
    return jnp.concatenate([first, second], axis=1)


def tap_table(filters, causal):
    width = filters.shape[1]
    rows = jnp.arange(width)[:, None]
    cols = jnp.arange(2 * width)[None, :]
    lag = rows + width - cols if causal else cols - rows
    valid = (lag >= 0) & (lag < width)
    index = jnp.clip(lag, 0, width - 1)
    table = filters[:, index]
    return jnp.where(valid[None], table, jnp.float32(0.0))


def convolve(extended, filters, skip_gain, causal):
    width = filters.shape[1]
    groups = filters.shape[0]
    channels = extended.shape[1]
    window = blocks_of(extended, width)
    count = window.shape[0]
    window = window.reshape(count, 2 * width, groups, channels // groups).astype(jnp.float32)
    mixed = jnp.einsum(
        "gij,bjgc->bigc", tap_table(filters, causal), window, precision=lax.Precision.HIGHEST
    )
    mixed = mixed.reshape(count * width, channels)
    current = extended[width:] if causal else extended[:-width]
    return mixed + skip_gain[None, :] * current.astype(jnp.float32)


def diagonal_lags(pairs, width):
    leading = pairs.shape[:-2]
    flat = pairs.reshape(leading + (width * 2 * width,))
    padded = jnp.concatenate([flat, jnp.zeros(leading + (width,), jnp.float32)], axis=-1)
    skewed = padded.reshape(leading + (width, 2 * width + 1)).sum(axis=-2)
    return skewed[..., width:0:-1]


def on_device(query_proj, key_proj, value_proj, filters, skip_gain, out_grad, w_out):
    width = filters.shape[1]
    groups = filters.shape[0]
    tok_rows = query_proj.shape[0]
    channels = query_proj.shape[1]
    span = channels // groups
    rim_rows = width - 1
    count = tok_rows // width
    query_f = query_proj.astype(jnp.float32)
    key_f = key_proj.astype(jnp.float32)
    value_f = value_proj.astype(jnp.float32)
    products = (key_f * value_f).astype(jnp.bfloat16)
    product_f = products.astype(jnp.float32)
    mixer_grad = lax.dot_general(
        lax.all_gather(out_grad, "tp", axis=1, tiled=True),
        w_out,
        (((1,), (1,)), ((), ())),
        preferred_element_type=jnp.float32,
    )
    earlier = passed_along(products[tok_rows - rim_rows :], "ctx", 1)
    single = jnp.zeros((1, channels), jnp.bfloat16)
    prod_ext = jnp.concatenate([single, earlier, products], axis=0)
    filtered = convolve(prod_ext, filters, skip_gain, True)
    query_grad = (mixer_grad * filtered).astype(jnp.bfloat16)
    filtered_grad = (mixer_grad * query_f).astype(jnp.bfloat16)
    grad_f = filtered_grad.astype(jnp.float32)
    later = passed_along(filtered_grad[:rim_rows], "ctx", -1)
    grad_ext = jnp.concatenate([filtered_grad, later, single], axis=0)
    product_grad = convolve(grad_ext, filters, skip_gain, False)
    key_grad = (product_grad * value_f).astype(jnp.bfloat16)
    value_grad = (product_grad * key_f).astype(jnp.bfloat16)
    window = blocks_of(prod_ext, width)
    grad_blocks = filtered_grad.reshape(count, width, channels)
    skip_part = jnp.sum(grad_f * product_f, axis=0)
    pairs = jnp.einsum(
        "bigc,bjgc->gij",
        grad_blocks.reshape(count, width, groups, span),
        window.reshape(count, 2 * width, groups, span),
        preferred_element_type=jnp.float32,
    )
    grouped = diagonal_lags(pairs, width)
    filter_grad, skip_grad = lax.psum((grouped, skip_part), "ctx")
    return (query_grad, key_grad, value_grad, filter_grad, skip_grad)


def solution(mesh):
    return jax.shard_map(
        on_device,
        mesh=mesh,
        in_specs=(
            P("ctx", "tp"),
            P("ctx", "tp"),
            P("ctx", "tp"),
            P("tp", None),
            P("tp"),
            P("ctx", "tp"),
            P("tp", None),
        ),
        out_specs=(P("ctx", "tp"), P("ctx", "tp"), P("ctx", "tp"), P("tp", None), P("tp")),
        check_vma=False,
    )
```

profile of v0, /device:TPU:0, one launch (start us, length us, event | category | flops | bytes accessed | tf_op | source)
XLA Modules:
  0.0 376.2 jit_solution(13880040861033989793)
XLA Ops:
  7.2 0.7 all-gather.2.cloned.1.call-update
  8.0 0.1 copy.37
  8.0 0.1 fusion.21
  8.1 0.1 copy.36
  8.3 20.7 %all-gather.2.cloned.1.call-done = bf16[128,4096]{1,0:T(8,128)(2,1)} async-done(((bf16[128,1024]{1,0:T(8,128)(2,1)}), bf16[128,4096]{1,0:T(8,128)(2,1)}) %all-gather.2.cloned.1.call-update) | async-done | bytes 1048592 | tf_op jit(solution)/shard_map/all_gather | solution.py:69
  29.0 6.7 %fusion.17 = (f32[1024]{0:T(1024)S(1)}, bf16[128,1024]{1,0:T(8,128)(2,1)S(1)}, bf16[128,1024]{1,0:T(8,128)(2,1)S(1)}, f32[128,1024]{1,0:T(8,128)S(1)}) fusion(bf16[128,1024]{1,0:T(8,128)(2,1)} %param.7, bf16[128,1024]{1,0:T(8,128)(2,1)} %param.9, bf16[128,1024]{1,0:T(8,128)(2,1)} %param.8, bf16[128,4096]{1,0:T(8,128)(2,1)} %all-gather.2.cloned.1.call-done, ...), kind=kOutput, calls=%fused_computation.25 | convolution fusion | flops 1075182592 | bytes 11276288 | tf_op jit(solution)/shard_map/dot_general | solution.py:68
  35.8 1.3 collective-permute-start.1
  37.1 0.1 copy.25
  37.2 108.4 %gather_fusion.1 = f32[32768,64]{1,0:T(8,128)} fusion(f32[64,128]{0,1:T(8,128)S(1)} %copy.25, s32[32768]{0:T(1024)S(1)} %broadcast_clamp_fusion), kind=kCustom, calls=%fused_computation.1 | custom fusion | bytes 16908288 | tf_op jit(solution)/shard_map/gather | solution.py:28
  145.6 13.6 %copy.31 = f32[128,256,64]{1,0,2:T(8,128)} copy(f32[128,256,64]{2,1,0:T(8,128)} %bitcast.45) | data formatting | bytes 16777216 | tf_op jit(solution)/shard_map/gather | solution.py:28
  159.2 108.3 %gather_fusion = f32[32768,64]{1,0:T(8,128)} fusion(f32[64,128]{0,1:T(8,128)S(1)} %copy.25, s32[32768]{0:T(1024)S(1)} %broadcast_clamp_fusion.1), kind=kCustom, calls=%fused_computation | custom fusion | bytes 16908288 | tf_op jit(solution)/shard_map/gather | solution.py:28
  267.5 13.6 %copy.26 = f32[128,256,64]{1,0,2:T(8,128)} copy(f32[128,256,64]{2,1,0:T(8,128)} %bitcast.44) | data formatting | bytes 16777216 | tf_op jit(solution)/shard_map/gather | solution.py:28
  281.1 0.1 fusion.27
  281.2 0.2 copy.28
  281.4 0.2 copy.24
  281.6 4.7 %collective-permute-start = (bf16[127,1024]{1,0:T(8,128)(2,1)S(1)}, bf16[127,1024]{1,0:T(8,128)(2,1)S(1)}, u32[]{:S(2)}, u32[]{:S(2)}) collective-permute-start(bf16[127,1024]{1,0:T(8,128)(2,1)S(1)} %slice.19), channel_id=1, source_target_pairs={{0,4},{4,8},{8,12},{12,16},{16,20},{20,24},{24,28},{1,5},{5,9},{9,... | collective-permute-start | bytes 780296 | tf_op jit(solution)/shard_map/ppermute | solution.py:10
  286.4 0.2 copy.35
  286.6 6.5 %fusion = f32[64,16,128]{2,1,0:T(8,128)S(1)} fusion(f32[128,256,64]{1,0,2:T(8,128)} %copy.31, pred[128,256]{1,0:T(8,128)(4,1)S(1)} %fusion.28, bf16[1,128,64,16]{1,3,2,0:T(8,128)(2,1)S(1)} %bitcast.57, bf16[1,128,64,16]{1,3,2,0:T(8,128)(2,1)S(1)} %bitcast.50), kind=kOutput, calls=%fused_computation.2 | convolution fusion | flops 405798912 | bytes 9469952 | tf_op jit(solution)/shard_map/gij,bjgc->bigc/dot_general | solution.py:39
  293.2 0.2 copy.32
  293.4 0.2 copy.34
  293.6 0.1 concatenate.27.clone
  293.7 6.5 %fusion.2 = f32[64,16,128]{2,1,0:T(8,128)S(1)} fusion(f32[128,256,64]{1,0,2:T(8,128)} %copy.26, pred[128,256]{1,0:T(8,128)(4,1)S(1)} %fusion.27, bf16[1,128,64,16]{1,3,2,0:T(8,128)(2,1)S(1)} %bitcast.52, bf16[1,128,64,16]{1,3,2,0:T(8,128)(2,1)S(1)} %bitcast.48), kind=kOutput, calls=%fused_computation.4 | convolution fusion | flops 405798912 | bytes 9469952 | tf_op jit(solution)/shard_map/gij,bjgc->bigc/dot_general | solution.py:39
  300.3 0.2 copy.27
  300.5 1.3 fusion.20
  301.8 4.7 %copy.38 = f32[8,8,128,256]{3,1,2,0:T(8,128)S(1)} copy(f32[8,8,128,256]{3,2,1,0:T(8,128)S(1)} %bitcast.47) | data formatting | bytes 16777216
  306.5 3.8 concatenate.35
  310.3 14.2 %reshape.171 = f32[64,128,257]{2,1,0:T(8,128)} reshape(f32[64,32896]{1,0:T(8,128)} %concatenate.35) | data formatting | bytes 16842752 | tf_op jit(solution)/shard_map/reshape | solution.py:51
  324.4 6.1 %reduce_sum.18 = f32[64,257]{1,0:T(8,128)S(1)} reduce(f32[64,128,257]{2,1,0:T(8,128)} %reshape.171, f32[]{:T(128)} %constant.1.clone.1), dimensions={1}, to_apply=%region_0.1 | reduce | flops 2088896 | bytes 8487172 | tf_op jit(solution)/shard_map/reduce_sum | solution.py:51
  330.6 0.1 slice.21
  330.7 0.1 rev.3
  330.7 37.5 %all-reduce.3 = (f32[64,128]{1,0:T(8,128)}, f32[1024]{0:T(1024)}) all-reduce(f32[64,128]{1,0:T(8,128)S(1)} %rev.3, f32[1024]{0:T(1024)S(1)} %get-tuple-element.7), channel_id=1, replica_groups=mesh['ctx'=8,'tp'=4] {'ctx'}, use_global_device_ids=true, to_apply=%region_1.2 | all-reduce | flops 9216 | bytes 73728 | tf_op jit(solution)/shard_map/psum | solution.py:96
  368.3 1.1 fusion.10
  (18 shorter events, 0.3 us)
Async XLA Ops:
  7.2 29.9 %copy-start.2 = (f32[64,128]{1,0:T(8,128)S(1)}, f32[64,128]{1,0:T(8,128)}, u32[]{:S(2)}) copy-start(f32[64,128]{1,0:T(8,128)} %param.10) | copy-start | bytes 98308
  7.2 21.9 %all-gather.2.cloned.1.call-start = ((), (), s32[]{:S(2)}) async-start(), calls=%async_computation | async-start | bytes 1310720 | tf_op jit(solution)/shard_map/all_gather | solution.py:69
  35.8 250.6 %collective-permute-start.1 = (bf16[127,1024]{1,0:T(8,128)(2,1)S(1)}, bf16[127,1024]{1,0:T(8,128)(2,1)S(1)}, u32[]{:S(2)}, u32[]{:S(2)}) collective-permute-start(bf16[127,1024]{1,0:T(8,128)(2,1)S(1)} %bitcast.54), channel_id=1, source_target_pairs={{4,0},{8,4},{12,8},{16,12},{20,16},{24,20},{28,24},{5,1},{9,5},{13... | collective-permute-start | bytes 780296 | tf_op jit(solution)/shard_map/ppermute | solution.py:10
  281.6 11.8 %collective-permute-start = (bf16[127,1024]{1,0:T(8,128)(2,1)S(1)}, bf16[127,1024]{1,0:T(8,128)(2,1)S(1)}, u32[]{:S(2)}, u32[]{:S(2)}) collective-permute-start(bf16[127,1024]{1,0:T(8,128)(2,1)S(1)} %slice.19), channel_id=1, source_target_pairs={{0,4},{4,8},{8,12},{12,16},{16,20},{20,24},{24,28},{1,5},{5,9},{9,... | collective-permute-start | bytes 780296 | tf_op jit(solution)/shard_map/ppermute | solution.py:10
  324.4 43.8 %copy-start = (bf16[128,1024]{1,0:T(8,128)(2,1)S(1)}, bf16[128,1024]{1,0:T(8,128)(2,1)}, u32[]{:S(2)}) copy-start(bf16[128,1024]{1,0:T(8,128)(2,1)} %param.8) | copy-start | bytes 786436
  324.4 43.8 %copy-start.1 = (bf16[128,1024]{1,0:T(8,128)(2,1)S(1)}, bf16[128,1024]{1,0:T(8,128)(2,1)}, u32[]{:S(2)}) copy-start(bf16[128,1024]{1,0:T(8,128)(2,1)} %param.9) | copy-start | bytes 786436
  324.4 43.8 %copy-start.3 = (f32[1024]{0:T(1024)S(1)}, f32[1024]{0:T(1024)}, u32[]{:S(2)}) copy-start(f32[1024]{0:T(1024)} %param.11) | copy-start | bytes 12292
Sparse Core Ops, SparseCore 0:
  9.6 19.4 all-gather.1
where the time goes:
time: 377 us; the launch traced here: 376 us
  local copies, waits for them, and re-layouts  268 us (71%)
  blocking collectives  37.5 us (10%)
  waiting for transfers between devices  21.4 us (6%)
  matrix products  21.1 us (6%)
  between operations  14.2 us (4%)
  other arithmetic  7.52 us (2%)
  starting transfers between devices  6.07 us (2%)
    gather x4, local copies, waits for them, and re-layouts, tap_table(): table = filters[:, index]  244 us
    psum x1, blocking collectives, on_device(): filter_grad, skip_grad = lax.psum((grouped, skip_part), 'ctx')  37.5 us
    all_gather x1, waiting for transfers between devices, on_device(): lax.all_gather(out_grad, 'tp', axis=1, tiled=True)  20.7 us
    reshape x1, local copies, waits for them, and re-layouts, diagonal_lags(): skewed = padded.reshape(leading + (width, 2 * width + 1)).sum(axis=-2)  14.2 us
    dot_general x2, matrix products, convolve(): jnp.einsum('gij,bjgc->bigc', tap_table(filters, causal), window, precisio...  13.1 us
  transfers between devices with their start and end apart: 3, of which 1 were waited for; matrix products, arithmetic and copies ran while one was open for 67% of the time, Pallas kernels for 0%

commit v1 on v0

--- a/solution.py
+++ b/solution.py
@@ -2,6 +2,27 @@
 import jax.numpy as jnp
 from jax import lax
 from jax.sharding import PartitionSpec as P
+
+
+def collect(shard, axis, dim):
+    length, position, rows = (lax.axis_size(axis), lax.axis_index(axis), shard.shape[dim])
+    right = [(i, (i + 1) % length) for i in range(length)]
+    backward = [(i, (i - 1) % length) for i in range(length)]
+    whole = jnp.zeros((*shard.shape[:dim], length * rows, *shard.shape[dim + 1 :]), shard.dtype)
+    whole = lax.dynamic_update_slice_in_dim(whole, shard, position * rows, axis=dim)
+    from_left = from_right = shard
+    middle = length // 2
+    for step in range(1, middle + 1):
+        from_left = lax.ppermute(from_left, axis, right)
+        whole = lax.dynamic_update_slice_in_dim(
+            whole, from_left, (position - step) % length * rows, axis=dim
+        )
+        if step < length - middle:
+            from_right = lax.ppermute(from_right, axis, backward)
+            whole = lax.dynamic_update_slice_in_dim(
+                whole, from_right, (position + step) % length * rows, axis=dim
+            )
+    return whole
 
 
 def passed_along(block, axis, distance):
@@ -66,7 +87,7 @@
     products = (key_f * value_f).astype(jnp.bfloat16)
     product_f = products.astype(jnp.float32)
     mixer_grad = lax.dot_general(
-        lax.all_gather(out_grad, "tp", axis=1, tiled=True),
+        collect(out_grad, "tp", 1),
         w_out,
         (((1,), (1,)), ((), ())),
         preferred_element_type=jnp.float32,

time: 377 us -> 359 us (0.952)
  waiting for transfers between devices: 21.4 us -> 5.95 us
  between operations: 14.2 us -> 0.95 us
  starting transfers between devices: 6.07 us -> 12.3 us
  local copies, waits for them, and re-layouts: 268 us -> 272 us
    all_gather x1 -> x0, waiting for transfers between devices: 20.7 us -> none  [on_device(): lax.all_gather(out_grad, 'tp', axis=1, tiled=True)]
    ppermute x0 -> x3, waiting for transfers between devices: none -> 5.95 us  [the longest x2 5.95 us: collect(): from_left = lax.ppermute(from_left, axis, right)]
    ppermute x0 -> x3, starting transfers between devices: none -> 5.11 us  [the longest x2 3.12 us: collect(): from_left = lax.ppermute(from_left, axis, right)]
  transfers between devices with their start and end apart: 3 -> 5, of which waited for: 1 -> 2; matrix products, arithmetic and copies ran while one was open for 67% -> 71% of each run, Pallas kernels for 0% -> 0%
where the time goes in v1:
time: 359 us; the launch traced here: 358 us
  local copies, waits for them, and re-layouts  272 us (76%)
  blocking collectives  38.4 us (11%)
  matrix products  20.7 us (6%)
  starting transfers between devices  12.3 us (3%)
  other arithmetic  7.55 us (2%)
  waiting for transfers between devices  5.95 us (2%)
    gather x4, local copies, waits for them, and re-layouts, tap_table(): table = filters[:, index]  245 us
    psum x1, blocking collectives, on_device(): filter_grad, skip_grad = lax.psum((grouped, skip_part), 'ctx')  38.4 us
    reshape x1, local copies, waits for them, and re-layouts, diagonal_lags(): skewed = padded.reshape(leading + (width, 2 * width + 1)).sum(axis=-2)  14.2 us
    dot_general x2, matrix products, convolve(): jnp.einsum('gij,bjgc->bigc', tap_table(filters, causal), window, precisio...  13.1 us
  transfers between devices with their start and end apart: 5, of which 2 were waited for; matrix products, arithmetic and copies ran while one was open for 71% of the time, Pallas kernels for 0%

profile of v1, /device:TPU:0, one launch (start us, length us, event | category | flops | bytes accessed | tf_op | source)
XLA Modules:
  0.0 358.1 jit_solution(17149208482503832707)
XLA Ops:
  0.6 0.5 collective-permute-start
  1.1 2.0 collective-permute-start.1
  3.3 0.1 fusion.21
  3.5 4.0 %collective-permute-done = bf16[128,1024]{1,0:T(8,128)(2,1)S(1)} collective-permute-done((bf16[128,1024]{1,0:T(8,128)(2,1)}, bf16[128,1024]{1,0:T(8,128)(2,1)S(1)}, u32[]{:S(2)}, u32[]{:S(2)}) %collective-permute-start) | collective-permute-done | bytes 262176 | tf_op jit(solution)/shard_map/ppermute | solution.py:16
  7.5 2.6 collective-permute-start.2
  10.2 1.0 constant_dynamic-update-slice_fusion.3
  11.3 2.0 collective-permute-done.2
  13.3 6.4 %fusion.17 = (f32[1024]{0:T(1024)S(1)}, bf16[128,1024]{1,0:T(8,128)(2,1)S(1)}, bf16[128,1024]{1,0:T(8,128)(2,1)S(1)}, f32[128,1024]{1,0:T(8,128)S(1)}) fusion(bf16[128,1024]{1,0:T(8,128)(2,1)} %param.7, bf16[128,1024]{1,0:T(8,128)(2,1)} %param.9, bf16[128,1024]{1,0:T(8,128)(2,1)} %param.8, bf16[128,4096]{1,0:T(8,128)(2,1)S(1)} %constant_dynamic-update-slice_fusion, ...), kind=kOutput, calls=%fused_computation.25 | convolution fusion | flops 1075182592 | bytes 11276288 | tf_op jit(solution)/shard_map/dot_general | solution.py:89
  19.7 1.3 collective-permute-start.4
  21.2 109.0 %gather_fusion.1 = f32[32768,64]{1,0:T(8,128)} fusion(f32[64,128]{0,1:T(8,128)S(1)} %copy.25, s32[32768]{0:T(1024)S(1)} %broadcast_clamp_fusion), kind=kCustom, calls=%fused_computation.1 | custom fusion | bytes 16908288 | tf_op jit(solution)/shard_map/gather | solution.py:49
  130.1 13.6 %copy.31 = f32[128,256,64]{1,0,2:T(8,128)} copy(f32[128,256,64]{2,1,0:T(8,128)} %bitcast.45) | data formatting | bytes 16777216 | tf_op jit(solution)/shard_map/gather | solution.py:49
  143.8 109.0 %gather_fusion = f32[32768,64]{1,0:T(8,128)} fusion(f32[64,128]{0,1:T(8,128)S(1)} %copy.25, s32[32768]{0:T(1024)S(1)} %broadcast_clamp_fusion.1), kind=kCustom, calls=%fused_computation | custom fusion | bytes 16908288 | tf_op jit(solution)/shard_map/gather | solution.py:49
  252.7 13.6 %copy.26 = f32[128,256,64]{1,0,2:T(8,128)} copy(f32[128,256,64]{2,1,0:T(8,128)} %bitcast.44) | data formatting | bytes 16777216 | tf_op jit(solution)/shard_map/gather | solution.py:49
  266.3 0.1 fusion.27
  266.5 0.2 copy.28
  266.6 0.2 copy.24
  266.8 0.8 slice.19
  267.6 5.9 %collective-permute-start.3 = (bf16[127,1024]{1,0:T(8,128)(2,1)}, bf16[127,1024]{1,0:T(8,128)(2,1)S(1)}, u32[]{:S(2)}, u32[]{:S(2)}) collective-permute-start(bf16[127,1024]{1,0:T(8,128)(2,1)} %slice.19), channel_id=1, source_target_pairs={{0,4},{4,8},{8,12},{12,16},{16,20},{20,24},{24,28},{1,5},{5,9},{9,... | collective-permute-start | bytes 780296 | tf_op jit(solution)/shard_map/ppermute | solution.py:31
  273.5 0.2 copy.35
  273.7 6.5 %fusion = f32[64,16,128]{2,1,0:T(8,128)S(1)} fusion(f32[128,256,64]{1,0,2:T(8,128)} %copy.31, pred[128,256]{1,0:T(8,128)(4,1)S(1)} %fusion.28, bf16[1,128,64,16]{1,3,2,0:T(8,128)(2,1)S(1)} %bitcast.57, bf16[1,128,64,16]{1,3,2,0:T(8,128)(2,1)S(1)} %bitcast.50), kind=kOutput, calls=%fused_computation.2 | convolution fusion | flops 405798912 | bytes 9469952 | tf_op jit(solution)/shard_map/gij,bjgc->bigc/dot_general | solution.py:60
  280.2 0.2 copy.32
  280.5 0.2 copy.34
  280.6 0.1 concatenate.27.clone
  280.8 6.5 %fusion.2 = f32[64,16,128]{2,1,0:T(8,128)S(1)} fusion(f32[128,256,64]{1,0,2:T(8,128)} %copy.26, pred[128,256]{1,0:T(8,128)(4,1)S(1)} %fusion.27, bf16[1,128,64,16]{1,3,2,0:T(8,128)(2,1)S(1)} %bitcast.52, bf16[1,128,64,16]{1,3,2,0:T(8,128)(2,1)S(1)} %bitcast.48), kind=kOutput, calls=%fused_computation.4 | convolution fusion | flops 405798912 | bytes 9469952 | tf_op jit(solution)/shard_map/gij,bjgc->bigc/dot_general | solution.py:60
  287.3 1.0 copy.27
  288.3 1.3 fusion.20
  289.6 4.7 %copy.38 = f32[8,8,128,256]{3,1,2,0:T(8,128)S(1)} copy(f32[8,8,128,256]{3,2,1,0:T(8,128)S(1)} %bitcast.47) | data formatting | bytes 16777216
  294.4 3.7 %concatenate.35 = f32[64,32896]{1,0:T(8,128)} pad(f32[64,32768]{1,0:T(8,128)S(1)} %bitcast.46, f32[]{:T(128)} %constant.48.clone.1), padding=0_0x0_128 | pad | bytes 16809988 | tf_op jit(solution)/shard_map/concatenate | solution.py:71
  298.1 14.2 %reshape.171 = f32[64,128,257]{2,1,0:T(8,128)} reshape(f32[64,32896]{1,0:T(8,128)} %concatenate.35) | data formatting | bytes 16842752 | tf_op jit(solution)/shard_map/reshape | solution.py:72
  312.3 6.2 %reduce_sum.18 = f32[64,257]{1,0:T(8,128)S(1)} reduce(f32[64,128,257]{2,1,0:T(8,128)} %reshape.171, f32[]{:T(128)} %constant.48.clone.1), dimensions={1}, to_apply=%region_0.1 | reduce | flops 2088896 | bytes 8487172 | tf_op jit(solution)/shard_map/reduce_sum | solution.py:72
  318.6 38.4 %all-reduce.3 = (f32[64,128]{1,0:T(8,128)}, f32[1024]{0:T(1024)}) all-reduce(f32[64,128]{1,0:T(8,128)S(1)} %rev.3, f32[1024]{0:T(1024)S(1)} %get-tuple-element.7), channel_id=1, replica_groups=mesh['ctx'=8,'tp'=4] {'ctx'}, use_global_device_ids=true, to_apply=%region_1.2 | all-reduce | flops 9216 | bytes 73728 | tf_op jit(solution)/shard_map/psum | solution.py:117
  357.0 1.1 fusion.10
  (28 shorter events, 0.7 us)
Async XLA Ops:
  0.6 20.4 %copy-start.3 = (f32[64,128]{1,0:T(8,128)S(1)}, f32[64,128]{1,0:T(8,128)}, u32[]{:S(2)}) copy-start(f32[64,128]{1,0:T(8,128)} %param.10) | copy-start | bytes 98308
  0.6 6.8 %collective-permute-start = (bf16[128,1024]{1,0:T(8,128)(2,1)}, bf16[128,1024]{1,0:T(8,128)(2,1)S(1)}, u32[]{:S(2)}, u32[]{:S(2)}) collective-permute-start(bf16[128,1024]{1,0:T(8,128)(2,1)} %param.12), channel_id=1, source_target_pairs={{0,1},{1,2},{2,3},{3,0},{4,5},{5,6},{6,7},{7,4},{8,9},{9,10},{10,1... | collective-permute-start | bytes 786440 | tf_op jit(solution)/shard_map/ppermute | solution.py:16
  1.1 10.1 %collective-permute-start.1 = (bf16[128,1024]{1,0:T(8,128)(2,1)}, bf16[128,1024]{1,0:T(8,128)(2,1)S(1)}, u32[]{:S(2)}, u32[]{:S(2)}) collective-permute-start(bf16[128,1024]{1,0:T(8,128)(2,1)} %param.12), channel_id=1, source_target_pairs={{0,3},{1,0},{2,1},{3,2},{4,7},{5,4},{6,5},{7,6},{8,11},{9,8},{10,9... | collective-permute-start | bytes 786440 | tf_op jit(solution)/shard_map/ppermute | solution.py:21
  7.5 5.8 %collective-permute-start.2 = (bf16[128,1024]{1,0:T(8,128)(2,1)S(1)}, bf16[128,1024]{1,0:T(8,128)(2,1)S(1)}, u32[]{:S(2)}, u32[]{:S(2)}) collective-permute-start(bf16[128,1024]{1,0:T(8,128)(2,1)S(1)} %collective-permute-done), channel_id=1, source_target_pairs={{0,1},{1,2},{2,3},{3,0},{4,5},{5,6},{6,7},{7,4},{8,9},{9,10},{10,1... | collective-permute-start | bytes 786440 | tf_op jit(solution)/shard_map/ppermute | solution.py:16
  19.7 253.7 %collective-permute-start.4 = (bf16[127,1024]{1,0:T(8,128)(2,1)S(1)}, bf16[127,1024]{1,0:T(8,128)(2,1)S(1)}, u32[]{:S(2)}, u32[]{:S(2)}) collective-permute-start(bf16[127,1024]{1,0:T(8,128)(2,1)S(1)} %bitcast.54), channel_id=1, source_target_pairs={{4,0},{8,4},{12,8},{16,12},{20,16},{24,20},{28,24},{5,1},{9,5},{13... | collective-permute-start | bytes 780296 | tf_op jit(solution)/shard_map/ppermute | solution.py:31
  267.6 12.9 %collective-permute-start.3 = (bf16[127,1024]{1,0:T(8,128)(2,1)}, bf16[127,1024]{1,0:T(8,128)(2,1)S(1)}, u32[]{:S(2)}, u32[]{:S(2)}) collective-permute-start(bf16[127,1024]{1,0:T(8,128)(2,1)} %slice.19), channel_id=1, source_target_pairs={{0,4},{4,8},{8,12},{12,16},{16,20},{20,24},{24,28},{1,5},{5,9},{9,... | collective-permute-start | bytes 780296 | tf_op jit(solution)/shard_map/ppermute | solution.py:31
  312.3 44.7 %copy-start = (f32[128,1024]{1,0:T(8,128)S(1)}, f32[128,1024]{1,0:T(8,128)}, u32[]{:S(2)}) copy-start(f32[128,1024]{1,0:T(8,128)} %copy.27) | copy-start | bytes 1572868
  312.3 44.7 %copy-start.1 = (bf16[128,1024]{1,0:T(8,128)(2,1)S(1)}, bf16[128,1024]{1,0:T(8,128)(2,1)}, u32[]{:S(2)}) copy-start(bf16[128,1024]{1,0:T(8,128)(2,1)} %param.8) | copy-start | bytes 786436
  312.3 44.7 %copy-start.2 = (bf16[128,1024]{1,0:T(8,128)(2,1)S(1)}, bf16[128,1024]{1,0:T(8,128)(2,1)}, u32[]{:S(2)}) copy-start(bf16[128,1024]{1,0:T(8,128)(2,1)} %param.9) | copy-start | bytes 786436
  312.3 44.7 %copy-start.4 = (f32[1024]{0:T(1024)S(1)}, f32[1024]{0:T(1024)}, u32[]{:S(2)}) copy-start(f32[1024]{0:T(1024)} %param.11) | copy-start | bytes 12292
